TPU v7x, 32 devices: a whole 2x2x4 slice. The times are simulated.
32 devices in a mesh: groups: 2 (over x), frame: 16 (over z, y, core).
Axes of the slice: x: 2, y: 2, z: 4, core: 2. Of those that a mesh axis runs over, the one named last changes fastest.
Arguments:
- query_in: bfloat16 [32, 512, 1536], P(('groups', 'frame')), parts along dimension 0, may hold values from -200 to 200, as said below
- keys_in: bfloat16 [32, 512, 1536], P(('groups', 'frame')), parts along dimension 0, may hold values from -7 to 7, as said below
- values_in: bfloat16 [32, 512, 1536], P(('groups', 'frame')), parts along dimension 0, may hold values from -6 to 6
- far_picks: int32 [32, 6], P('groups'), parts along dimension 0, may hold values from 0 to 3
- win_rows: int32 [32], P(('groups', 'frame')), parts along dimension 0, may hold values from 1 to 15, as said below
Outputs:
- attended: bfloat16 [32, 512, 1536], P(('groups', 'frame')), parts along dimension 0
There are 2 independent parts, one for each index of `groups`. A program takes and returns all parts, laid end to end along the dimension named above; each array names one. Nothing has to cross between parts.
Inputs may be any that keep to these rules, and one draw needn't show every extreme that they name: `query_in`: entries of the queries lie within this range. `keys_in`: entries of the keys lie within this range. `win_rows`: every draw has a frame with window 1 and a frame with window 16 - 1.
All inputs are finite; a program needn't handle non-finite values.
Results may differ from a plain program's by a relative error of at most 0.0032.
Values may be sent and summed in bfloat16 or wider, within the bound.
A program may use at most 128 MiB of HBM per device.

v0:
```python
import math

import jax
import jax.numpy as jnp
from jax import lax
from jax.sharding import PartitionSpec as P

HD = 128
COLS = 32
SUB = 128
NREACH = 3


def with_halo(block, sides, width):
    for axis, dim in sides:
        count = lax.axis_size(axis)
        forward = [(i, i + 1) for i in range(count - 1)]
        backward = [(target, source) for source, target in forward]
        low = lax.ppermute(
            lax.slice_in_dim(block, block.shape[dim] - width, None, axis=dim), axis, forward
        )
        high = lax.ppermute(lax.slice_in_dim(block, 0, width, axis=dim), axis, backward)
        block = jnp.concatenate([low, block, high], axis=dim)
    return block


def from_behind(value, axis, steps):
    count = lax.axis_size(axis)
    leading, last = (max(0, -steps), min(count, count - steps))
    return lax.ppermute(value, axis, [(source, source + steps) for source in range(leading, last)])


def offsets_for(frames):
    spacing = [frames // 2 ** (NREACH - level_index) for level_index in range(NREACH)]
    return [-stride for stride in spacing] + [stride for stride in spacing]


def build_mask(window, frame_ok, far_ok, tokens_count):
    query_rows = jnp.arange(tokens_count, dtype=jnp.int32) // COLS
    key_rows = jnp.tile(query_rows, 3)
    nearby = jnp.abs(query_rows[:, None] - key_rows[None, :]) <= window
    nearby = nearby & jnp.repeat(frame_ok, tokens_count)[None, :]
    distant = jnp.repeat(far_ok, SUB)[None, :]
    distant = jnp.broadcast_to(distant, (tokens_count, distant.shape[1]))
    return jnp.concatenate([nearby, distant], axis=1)


def attend(queries, key_value, allowed):
    tokens_count = queries.shape[0]
    model_width = queries.shape[1]
    heads_count = model_width // HD

    def split_heads(matrix):
        return matrix.reshape(matrix.shape[0], heads_count, HD).transpose(1, 0, 2)

    query_heads = split_heads(queries)
    key_heads = split_heads(key_value[:, :model_width])
    value_heads = split_heads(key_value[:, model_width:])

    def one_head(operands):
        query_head, key_head, value_head = operands
        scores = lax.dot_general(
            query_head, key_head, (((1,), (1,)), ((), ())), preferred_element_type=jnp.float32
        )
        scores = scores * (1.0 / math.sqrt(HD))
        scores = jnp.where(allowed, scores, -1e30)
        row_peak = jnp.max(scores, axis=1, keepdims=True)
        raw_weights = jnp.exp(scores - row_peak)
        row_total = jnp.sum(raw_weights, axis=1, keepdims=True)
        weighted = jnp.dot(
            raw_weights.astype(jnp.bfloat16), value_head, preferred_element_type=jnp.float32
        )
        return weighted / row_total

    heads_out = lax.map(one_head, (query_heads, key_heads, value_heads))
    return heads_out.transpose(1, 0, 2).reshape(tokens_count, model_width).astype(jnp.bfloat16)


def body(query_in, keys_in, values_in, far_picks, win_rows):
    frames = lax.axis_size("frame")
    position = lax.axis_index("frame")
    tokens_count = query_in.shape[1]
    model_width = query_in.shape[2]
    key_value = jnp.concatenate([keys_in[0], values_in[0]], axis=1)
    beside_all = with_halo(key_value[None], (("frame", 0),), 1)
    beside_all = beside_all.reshape(3 * tokens_count, 2 * model_width)
    offsets = offsets_for(frames)
    offset_list = jnp.array(offsets, dtype=jnp.int32)
    blocks = key_value.reshape(tokens_count // SUB, SUB, 2 * model_width)
    pieces = []
    for column, offset in enumerate(offsets):
        reader = jnp.clip(position - offset, 0, frames - 1)
        chosen = lax.dynamic_index_in_dim(blocks, far_picks[reader, column], 0, keepdims=False)
        pieces.append(from_behind(chosen, "frame", -offset))
    distant = jnp.stack(pieces).reshape(len(offsets) * SUB, 2 * model_width)
    frame_ok = jnp.stack([position >= 1, position >= 0, position + 1 < frames])
    far_ok = (position + offset_list >= 0) & (position + offset_list < frames)
    allowed = build_mask(win_rows[0], frame_ok, far_ok, tokens_count)
    key_all = jnp.concatenate([beside_all, distant], axis=0)
    return attend(query_in[0], key_all, allowed)[None]


def solution(mesh):
    in_specs = (
        P(("groups", "frame"), None, None),
        P(("groups", "frame"), None, None),
        P(("groups", "frame"), None, None),
        P("groups", None),
        P(("groups", "frame")),
    )
    out_specs = P(("groups", "frame"), None, None)
    return jax.shard_map(body, mesh=mesh, in_specs=in_specs, out_specs=out_specs, check_vma=False)
```

profile of v0, /device:TPU:1, one launch (start us, length us, event | category | flops | bytes accessed | tf_op | source)
XLA Modules:
  0.0 246.2 jit_solution(5219857115101197629)
XLA Ops:
  0.0 4.0 %maximum_bitcast_fusion = bf16[1,512,3072]{2,1,0:T(8,128)(2,1)} fusion(bf16[512,1536]{1,0:T(8,128)(2,1)} %bitcast.89, bf16[512,1536]{1,0:T(8,128)(2,1)} %bitcast.87), kind=kLoop, calls=%fused_computation.36 | loop fusion | flops 6291456 | bytes 6291456 | tf_op jit(solution)/shard_map/broadcast_in_dim | solution.py:85
  4.0 4.5 %collective-permute-start = (bf16[1,512,3072]{2,1,0:T(8,128)(2,1)}, bf16[1,512,3072]{2,1,0:T(8,128)(2,1)}, u32[]{:S(2)}, u32[]{:S(2)}) collective-permute-start(bf16[1,512,3072]{2,1,0:T(8,128)(2,1)} %maximum_bitcast_fusion), channel_id=1, source_target_pairs={{0,1},{1,2},{2,3},{3,4},{4,5},{5,6},{6,7},{7,8},{8,9},{9,10},{10,1... | collective-permute-start | bytes 9437192 | tf_op jit(solution)/shard_map/ppermute | solution.py:19
  8.5 1.9 collective-permute-start.1
  10.5 0.7 constant_dynamic-slice_fusion.2
  22.7 2.2 fusion.23
  25.0 4.0 %collective-permute-start.2 = (bf16[128,3072]{1,0:T(8,128)(2,1)}, bf16[128,3072]{1,0:T(8,128)(2,1)}, u32[]{:S(2)}, u32[]{:S(2)}) collective-permute-start(bf16[128,3072]{1,0:T(8,128)(2,1)} %get-tuple-element.67), channel_id=1, source_target_pairs={{0,2},{1,3},{2,4},{3,5},{4,6},{5,7},{6,8},{7,9},{8,10},{9,11},{10,... | collective-permute-start | bytes 2359304 | tf_op jit(solution)/shard_map/ppermute | solution.py:30
  29.0 3.2 %collective-permute-start.3 = (bf16[128,3072]{1,0:T(8,128)(2,1)}, bf16[128,3072]{1,0:T(8,128)(2,1)}, u32[]{:S(2)}, u32[]{:S(2)}) collective-permute-start(bf16[128,3072]{1,0:T(8,128)(2,1)} %get-tuple-element.68), channel_id=1, source_target_pairs={{0,4},{1,5},{2,6},{3,7},{4,8},{5,9},{6,10},{7,11},{8,12},{9,13},{1... | collective-permute-start | bytes 2359304 | tf_op jit(solution)/shard_map/ppermute | solution.py:30
  32.2 4.7 %collective-permute-start.4 = (bf16[128,3072]{1,0:T(8,128)(2,1)}, bf16[128,3072]{1,0:T(8,128)(2,1)}, u32[]{:S(2)}, u32[]{:S(2)}) collective-permute-start(bf16[128,3072]{1,0:T(8,128)(2,1)} %get-tuple-element.69), channel_id=1, source_target_pairs={{0,8},{1,9},{2,10},{3,11},{4,12},{5,13},{6,14},{7,15},{16,24},{17,... | collective-permute-start | bytes 2359304 | tf_op jit(solution)/shard_map/ppermute | solution.py:30
  37.8 1.0 fusion.21
  39.4 1.7 copy.21
  41.2 60.8 %collective-permute-done.2 = bf16[128,3072]{1,0:T(8,128)(2,1)} collective-permute-done((bf16[128,3072]{1,0:T(8,128)(2,1)}, bf16[128,3072]{1,0:T(8,128)(2,1)}, u32[]{:S(2)}, u32[]{:S(2)}) %collective-permute-start.2) | collective-permute-done | bytes 786464 | tf_op jit(solution)/shard_map/ppermute | solution.py:30
  102.0 1.3 collective-permute-start.5
  103.3 1.2 bitcast_dynamic-update-slice_fusion.5
  104.5 1.3 collective-permute-start.6
  105.8 1.2 bitcast_dynamic-update-slice_fusion.4
  107.0 1.3 collective-permute-start.7
  108.3 1.2 bitcast_dynamic-update-slice_fusion.3
  109.5 5.9 %collective-permute-done.5 = bf16[128,3072]{1,0:T(8,128)(2,1)S(1)} collective-permute-done((bf16[128,3072]{1,0:T(8,128)(2,1)}, bf16[128,3072]{1,0:T(8,128)(2,1)S(1)}, u32[]{:S(2)}, u32[]{:S(2)}) %collective-permute-start.5) | collective-permute-done | bytes 786464 | tf_op jit(solution)/shard_map/ppermute | solution.py:30
  115.5 9.5 %collective-permute-done.6 = bf16[128,3072]{1,0:T(8,128)(2,1)S(1)} collective-permute-done((bf16[128,3072]{1,0:T(8,128)(2,1)}, bf16[128,3072]{1,0:T(8,128)(2,1)S(1)}, u32[]{:S(2)}, u32[]{:S(2)}) %collective-permute-start.6) | collective-permute-done | bytes 786464 | tf_op jit(solution)/shard_map/ppermute | solution.py:30
  125.1 17.8 %collective-permute-done.7 = bf16[128,3072]{1,0:T(8,128)(2,1)S(1)} collective-permute-done((bf16[128,3072]{1,0:T(8,128)(2,1)S(1)}, bf16[128,3072]{1,0:T(8,128)(2,1)S(1)}, u32[]{:S(2)}, u32[]{:S(2)}) %collective-permute-start.7) | collective-permute-done | bytes 786464 | tf_op jit(solution)/shard_map/ppermute | solution.py:30
  143.0 5.2 %pad_maximum_fusion = bf16[3,512,3072]{2,1,0:T(8,128)(2,1)S(1)} fusion(bf16[1,512,3072]{2,1,0:T(8,128)(2,1)} %collective-permute-done.1, bf16[1,512,3072]{2,1,0:T(8,128)(2,1)} %maximum_bitcast_fusion, bf16[1,512,3072]{2,1,0:T(8,128)(2,1)} %collective-permute-done), kind=kLoop, calls=%fused_computation.20 | loop fusion | flops 9437184 | bytes 18874368 | tf_op jit(solution)/shard_map/concatenate | solution.py:23
  148.2 6.2 %pad_maximum_fusion.1 = (bf16[2304,1536]{1,0:T(8,128)(2,1)}, bf16[2304,1536]{1,0:T(8,128)(2,1)}) fusion(bf16[768,3072]{1,0:T(8,128)(2,1)S(1)} %bitcast.86, bf16[1536,3072]{1,0:T(8,128)(2,1)S(1)} %bitcast.83), kind=kLoop, calls=%fused_computation.22 | loop fusion | flops 28311552 | bytes 28311552 | tf_op jit(solution)/shard_map/concatenate | solution.py:99
  154.4 10.4 %copy.22 = bf16[2304,1536]{0,1:T(8,128)(2,1)} copy(bf16[2304,1536]{1,0:T(8,128)(2,1)} %get-tuple-element.65) | data formatting | bytes 14155776 | tf_op jit(solution)/shard_map/slice | solution.py:57
  164.8 9.8 %copy.23 = bf16[2304,1536]{0,1:T(8,128)(2,1)} copy(bf16[2304,1536]{1,0:T(8,128)(2,1)} %get-tuple-element.64) | data formatting | bytes 14155776 | tf_op jit(solution)/shard_map/slice | solution.py:58
  174.6 69.1 %while.10 = (s32[]{:T(128)}, bf16[12,512,128]{1,2,0:T(8,128)(2,1)}, bf16[12,512,128]{1,2,0:T(8,128)(2,1)S(1)}, bf16[12,2304,128]{1,2,0:T(8,128)(2,1)}, pred[512,...) while((s32[]{:T(128)}, bf16[12,512,128]{1,2,0:T(8,128)(2,1)}, ...), condition=%wide.region_3.4_spmd, body=%wide.region_0.3_spmd.sunk | while | flops 612367360 | bytes 17313868 | solution.py:75
  174.6 2.2 fusion.45
  176.9 0.8 fusion.46
  177.6 1.9 fusion.47
  180.4 2.2 fusion.45
  182.6 0.8 fusion.46
  183.4 1.9 fusion.47
  186.1 2.2 fusion.45
  188.3 0.8 fusion.46
  189.1 1.9 fusion.47
  191.2 0.7 constant_dynamic-update-slice_fusion.2
  191.9 2.2 fusion.45
  194.1 0.8 fusion.46
  194.9 1.9 fusion.47
  197.6 2.2 fusion.45
  199.9 0.8 fusion.46
  200.6 1.9 fusion.47
  202.7 0.7 constant_dynamic-update-slice_fusion.2
  203.4 2.2 fusion.45
  205.6 0.8 fusion.46
  206.4 1.9 fusion.47
  209.1 2.2 fusion.45
  211.4 0.8 fusion.46
  212.2 1.9 fusion.47
  214.9 2.2 fusion.45
  217.1 0.8 fusion.46
  217.9 1.9 fusion.47
  220.6 2.2 fusion.45
  222.9 0.8 fusion.46
  223.7 1.9 fusion.47
  226.4 2.2 fusion.45
  228.6 0.8 fusion.46
  229.4 1.9 fusion.47
  232.2 2.2 fusion.45
  234.4 0.8 fusion.46
  235.2 1.9 fusion.47
  237.9 2.2 fusion.45
  240.1 0.8 fusion.46
  240.9 1.9 fusion.47
  243.7 2.6 %copy.28 = bf16[1,512,1536]{2,1,0:T(8,128)(2,1)} copy(bf16[1,512,1536]{1,2,0:T(8,128)(2,1)} %bitcast.92) | data formatting | bytes 3145728 | tf_op jit(solution)/shard_map/convert_element_type | solution.py:76
  (50 shorter events, 9.0 us)
Async XLA Ops:
  0.0 10.5 %copy-start.3 = (s32[16,6]{0,1:T(8,128)S(1)}, s32[16,6]{0,1:T(8,128)}, u32[]{:S(2)}) copy-start(s32[16,6]{0,1:T(8,128)} %param.11) | copy-start | bytes 1156
  0.0 22.7 %copy-start = (bf16[1,512,1536]{2,1,0:T(8,128)(2,1)S(1)}, bf16[1,512,1536]{2,1,0:T(8,128)(2,1)}, u32[]{:S(2)}) copy-start(bf16[1,512,1536]{2,1,0:T(8,128)(2,1)} %param.9) | copy-start | bytes 4718596
  0.0 22.7 %copy-start.1 = (bf16[1,512,1536]{2,1,0:T(8,128)(2,1)S(1)}, bf16[1,512,1536]{2,1,0:T(8,128)(2,1)}, u32[]{:S(2)}) copy-start(bf16[1,512,1536]{2,1,0:T(8,128)(2,1)} %param.10) | copy-start | bytes 4718596
  4.0 138.9 %collective-permute-start = (bf16[1,512,3072]{2,1,0:T(8,128)(2,1)}, bf16[1,512,3072]{2,1,0:T(8,128)(2,1)}, u32[]{:S(2)}, u32[]{:S(2)}) collective-permute-start(bf16[1,512,3072]{2,1,0:T(8,128)(2,1)} %maximum_bitcast_fusion), channel_id=1, source_target_pairs={{0,1},{1,2},{2,3},{3,4},{4,5},{5,6},{6,7},{7,8},{8,9},{9,10},{10,1... | collective-permute-start | bytes 9437192 | tf_op jit(solution)/shard_map/ppermute | solution.py:19
  8.5 134.4 %collective-permute-start.1 = (bf16[1,512,3072]{2,1,0:T(8,128)(2,1)}, bf16[1,512,3072]{2,1,0:T(8,128)(2,1)}, u32[]{:S(2)}, u32[]{:S(2)}) collective-permute-start(bf16[1,512,3072]{2,1,0:T(8,128)(2,1)} %maximum_bitcast_fusion), channel_id=1, source_target_pairs={{1,0},{2,1},{3,2},{4,3},{5,4},{6,5},{7,6},{8,7},{9,8},{10,9},{11,1... | collective-permute-start | bytes 9437192 | tf_op jit(solution)/shard_map/ppermute | solution.py:22
  22.7 15.1 %copy-start.4 = (s32[6]{0:T(128)S(1)}, s32[6]{0:T(128)}, u32[]{:S(2)}) copy-start(s32[6]{0:T(128)} %constant.97.clone) | copy-start | bytes 76
  25.0 77.0 %collective-permute-start.2 = (bf16[128,3072]{1,0:T(8,128)(2,1)}, bf16[128,3072]{1,0:T(8,128)(2,1)}, u32[]{:S(2)}, u32[]{:S(2)}) collective-permute-start(bf16[128,3072]{1,0:T(8,128)(2,1)} %get-tuple-element.67), channel_id=1, source_target_pairs={{0,2},{1,3},{2,4},{3,5},{4,6},{5,7},{6,8},{7,9},{8,10},{9,11},{10,... | collective-permute-start | bytes 2359304 | tf_op jit(solution)/shard_map/ppermute | solution.py:30
  29.0 75.5 %collective-permute-start.3 = (bf16[128,3072]{1,0:T(8,128)(2,1)}, bf16[128,3072]{1,0:T(8,128)(2,1)}, u32[]{:S(2)}, u32[]{:S(2)}) collective-permute-start(bf16[128,3072]{1,0:T(8,128)(2,1)} %get-tuple-element.68), channel_id=1, source_target_pairs={{0,4},{1,5},{2,6},{3,7},{4,8},{5,9},{6,10},{7,11},{8,12},{9,13},{1... | collective-permute-start | bytes 2359304 | tf_op jit(solution)/shard_map/ppermute | solution.py:30
  32.2 74.8 %collective-permute-start.4 = (bf16[128,3072]{1,0:T(8,128)(2,1)}, bf16[128,3072]{1,0:T(8,128)(2,1)}, u32[]{:S(2)}, u32[]{:S(2)}) collective-permute-start(bf16[128,3072]{1,0:T(8,128)(2,1)} %get-tuple-element.69), channel_id=1, source_target_pairs={{0,8},{1,9},{2,10},{3,11},{4,12},{5,13},{6,14},{7,15},{16,24},{17,... | collective-permute-start | bytes 2359304 | tf_op jit(solution)/shard_map/ppermute | solution.py:30
  41.2 65.8 %copy-start.2 = (bf16[128,3072]{1,0:T(8,128)(2,1)S(1)}, bf16[128,3072]{1,0:T(8,128)(2,1)}, u32[]{:S(2)}) copy-start(bf16[128,3072]{1,0:T(8,128)(2,1)} %get-tuple-element.66) | copy-start | bytes 2359300
  102.0 13.4 %collective-permute-start.5 = (bf16[128,3072]{1,0:T(8,128)(2,1)}, bf16[128,3072]{1,0:T(8,128)(2,1)S(1)}, u32[]{:S(2)}, u32[]{:S(2)}) collective-permute-start(bf16[128,3072]{1,0:T(8,128)(2,1)} %get-tuple-element.70), channel_id=1, source_target_pairs={{2,0},{3,1},{4,2},{5,3},{6,4},{7,5},{8,6},{9,7},{10,8},{11,9},{12,... | collective-permute-start | bytes 2359304 | tf_op jit(solution)/shard_map/ppermute | solution.py:30
  104.5 20.5 %collective-permute-start.6 = (bf16[128,3072]{1,0:T(8,128)(2,1)}, bf16[128,3072]{1,0:T(8,128)(2,1)S(1)}, u32[]{:S(2)}, u32[]{:S(2)}) collective-permute-start(bf16[128,3072]{1,0:T(8,128)(2,1)} %get-tuple-element.71), channel_id=1, source_target_pairs={{4,0},{5,1},{6,2},{7,3},{8,4},{9,5},{10,6},{11,7},{12,8},{13,9},{1... | collective-permute-start | bytes 2359304 | tf_op jit(solution)/shard_map/ppermute | solution.py:30
  107.0 35.9 %collective-permute-start.7 = (bf16[128,3072]{1,0:T(8,128)(2,1)S(1)}, bf16[128,3072]{1,0:T(8,128)(2,1)S(1)}, u32[]{:S(2)}, u32[]{:S(2)}) collective-permute-start(bf16[128,3072]{1,0:T(8,128)(2,1)S(1)} %copy-done.2), channel_id=1, source_target_pairs={{8,0},{9,1},{10,2},{11,3},{12,4},{13,5},{14,6},{15,7},{24,16},{25,... | collective-permute-start | bytes 2359304 | tf_op jit(solution)/shard_map/ppermute | solution.py:30
where the time goes:
time: 248 us; the launch traced here: 246 us
  waiting for transfers between devices  94.1 us (38%)
  matrix products  50.1 us (20%)
  local copies, waits for them, and re-layouts  38.5 us (16%)
  other arithmetic  28.6 us (12%)
  starting transfers between devices  22.3 us (9%)
  between operations  12.4 us (5%)
    ppermute x6, waiting for transfers between devices, from_behind(): lax.ppermute(value, axis, [(source, source + steps) for source in range(l...  94.1 us
    dot_general x12, matrix products, one_head(): lax.dot_general(query_head, key_head, (((1,), (1,)), ((), ())), preferred...  26.9 us
    dot_general x12, matrix products, one_head(): jnp.dot(raw_weights.astype(jnp.bfloat16), value_head, preferred_element_t...  23.2 us
    ppermute x6, starting transfers between devices, from_behind(): lax.ppermute(value, axis, [(source, source + steps) for source in range(l...  15.9 us
    slice x1, local copies, waits for them, and re-layouts, attend(): key_heads = split_heads(key_value[:, :model_width])  10.4 us
    slice x1, local copies, waits for them, and re-layouts, attend(): value_heads = split_heads(key_value[:, model_width:])  9.81 us
    dynamic_update_slice x24, local copies, waits for them, and re-layouts, attend(): heads_out = lax.map(one_head, (query_heads, key_heads, value_heads))  9.43 us
    reduce_sum x12, other arithmetic, one_head(): row_total = jnp.sum(raw_weights, axis=1, keepdims=True)  9.34 us
  transfers between devices with their start and end apart: 8, of which 4 were waited for; matrix products, arithmetic and copies ran while one was open for 4% of the time, Pallas kernels for 0%

commit v1 on v0

v1 whole, which is shorter than its diff:
```python
import functools
import math

import jax
import jax.numpy as jnp
from jax import lax
from jax.experimental import pallas as pl
from jax.experimental.pallas import tpu as pltpu
from jax.sharding import PartitionSpec as P

HD = 128
COLS = 32
SUB = 128
NREACH = 3
NEG = -1e30
CHUNKS = 3
TILE = 256
FACTOR = math.log2(math.e) / math.sqrt(HD)


def kernel(
    frames, q_hbm, k_hbm, v_hbm, picks, win, out_ref,
    qs, ks, vs, near_k, near_v, stage_k, stage_v, far_k, far_v,
    peak, total, acc, bias,
    in_sem, near_send, near_recv, far_send, far_recv,
):
    tokens, width = qs.shape
    heads = width // HD
    part = width // CHUNKS
    part_heads = heads // CHUNKS
    group = lax.axis_index("groups")
    me = lax.axis_index("frame")
    steps = [frames // 2 ** (NREACH - j) for j in range(NREACH)]

    def device(index):
        return (group, index)

    far_offsets = [-steps[0], steps[0], -steps[1], steps[1]]

    def inside(index):
        return (index >= 0) & (index < frames)

    partners = [-1, 1] + far_offsets + [-steps[2], steps[2]]

    loads = [
        pltpu.make_async_copy(src, dst, in_sem.at[i])
        for i, (src, dst) in enumerate(((k_hbm.at[0], ks), (v_hbm.at[0], vs), (q_hbm.at[0], qs)))
    ]
    for load in loads:
        load.start()

    barrier = pltpu.get_barrier_semaphore()
    count = jnp.int32(0)
    for offset in partners:
        ok = inside(me + offset)
        count = count + ok.astype(jnp.int32)

        @pl.when(ok)
        def _():
            pl.semaphore_signal(
                barrier, inc=1, device_id=device(me + offset), device_id_type=pl.DeviceIdType.MESH
            )
    pl.semaphore_wait(barrier, count)

    def near_copy(side, chunk, kind):
        target = me + 1 if side == 0 else me - 1
        src = (k_hbm, v_hbm)[kind].at[0, :, pl.ds(chunk * part, part)]
        dst = (near_k, near_v)[kind].at[side, :, pl.ds(chunk * part, part)]
        return pltpu.make_async_remote_copy(
            src_ref=src, dst_ref=dst,
            send_sem=near_send.at[side, chunk, kind], recv_sem=near_recv.at[side, chunk, kind],
            device_id=device(target), device_id_type=pl.DeviceIdType.MESH,
        )

    def each_near(action):
        for chunk in range(CHUNKS):
            for side in range(2):
                @pl.when(inside(me + 1 if side == 0 else me - 1))
                def _():
                    for kind in range(2):
                        action(near_copy(side, chunk, kind))

    each_near(lambda copy: copy.start())

    loads[0].wait()
    loads[1].wait()

    def far_copy(slot, offset, kind):
        rows = pl.ds(slot * SUB, SUB)
        return pltpu.make_async_remote_copy(
            src_ref=(stage_k, stage_v)[kind].at[rows, :], dst_ref=(far_k, far_v)[kind].at[rows, :],
            send_sem=far_send.at[slot, kind], recv_sem=far_recv.at[slot, kind],
            device_id=device(me - offset), device_id_type=pl.DeviceIdType.MESH,
        )

    long_slot = len(far_offsets)

    def stage(slot, pick):
        chosen = jnp.broadcast_to(pick, (16, HD))
        hot = [
            jnp.concatenate(
                [jnp.where(chosen == block, 1.0, 0.0).astype(stage_k.dtype)] * (SUB // 16), axis=0
            )
            for block in range(tokens // SUB)
        ]

        def one_head(head, carry):
            columns = pl.ds(pl.multiple_of(head * HD, HD), HD)
            for src, dst in ((ks, stage_k), (vs, stage_v)):
                mixed = hot[0] * src[pl.ds(0, SUB), columns]
                for block in range(1, tokens // SUB):
                    mixed = mixed + hot[block] * src[pl.ds(block * SUB, SUB), columns]
                dst[pl.ds(slot * SUB, SUB), columns] = mixed
            return carry
        lax.fori_loop(0, heads, one_head, 0)
    sends = [
        (long_slot, -steps[2], NREACH - 1), (long_slot, steps[2], 2 * NREACH - 1),
        (2, -steps[1], 1), (3, steps[1], NREACH + 1),
        (0, -steps[0], 0), (1, steps[0], NREACH),
    ]
    for slot, offset, column in sends:
        @pl.when(inside(me - offset))
        def _():
            stage(slot, picks[me - offset, column])
            far_copy(slot, offset, 0).start()
            far_copy(slot, offset, 1).start()

    for slot, offset in enumerate(far_offsets):
        @pl.when(jnp.logical_not(inside(me + offset)))
        def _():
            rows = pl.ds(slot * SUB, SUB)
            far_k[rows, :] = jnp.zeros((SUB, width), far_k.dtype)
            far_v[rows, :] = jnp.zeros((SUB, width), far_v.dtype)

    reach = jnp.broadcast_to(win[0], (tokens, tokens))
    query_row = lax.broadcasted_iota(jnp.int32, (tokens, tokens), 0) // COLS
    key_row = lax.broadcasted_iota(jnp.int32, (tokens, tokens), 1) // COLS
    bias[...] = jnp.where(jnp.abs(query_row - key_row) <= reach, 0.0, NEG)
    loads[2].wait()

    def update(head, tile, key, value, shift, first, last):
        columns = pl.ds(pl.multiple_of(head * HD, HD), HD)
        rows = pl.ds(tile * TILE, TILE)
        scores = lax.dot_general(
            qs[rows, columns], key, (((1,), (1,)), ((), ())), preferred_element_type=jnp.float32
        )
        if shift is not None:
            scores = scores + shift
        lanes = scores.shape[1] // HD
        high = jnp.broadcast_to(jnp.max(scores, axis=1, keepdims=True), (TILE, HD))
        if not first:
            old = peak[head, rows, :]
            high = jnp.maximum(old, high)
            fade = jnp.exp2((old - high) * FACTOR)
        raw = jnp.exp2((scores - jnp.concatenate([high] * lanes, axis=1)) * FACTOR)
        summed = raw[:, :HD]
        for lane in range(1, lanes):
            summed = summed + raw[:, lane * HD:(lane + 1) * HD]
        weighted = jnp.dot(raw.astype(jnp.bfloat16), value, preferred_element_type=jnp.float32)
        if not first:
            summed = summed + fade * total[head, rows, :]
            weighted = weighted + fade * acc[rows, columns]
        if last:
            row_total = jnp.sum(summed, axis=1, keepdims=True)
            out_ref[0, rows, columns] = (weighted / row_total).astype(out_ref.dtype)
        else:
            peak[head, rows, :] = high
            total[head, rows, :] = summed
            acc[rows, columns] = weighted

    def sweep(low, high, keys, values, shift_for, first=False, last=False):
        def one_head(head, carry):
            columns = pl.ds(pl.multiple_of(head * HD, HD), HD)
            key, value = keys(columns), values(columns)
            for tile in range(tokens // TILE):
                update(head, tile, key, value, shift_for(tile), first, last)
            return carry
        lax.fori_loop(low, high, one_head, 0)

    def near_bias(tile):
        return bias[pl.ds(tile * TILE, TILE), :]

    sweep(0, heads, lambda c: ks[:, c], lambda c: vs[:, c], near_bias, first=True)

    for chunk in range(CHUNKS):
        for side in range(2):
            @pl.when(inside(me - 1 if side == 0 else me + 1))
            def _():
                near_copy(side, chunk, 0).wait_recv()
                near_copy(side, chunk, 1).wait_recv()
                sweep(
                    chunk * part_heads, (chunk + 1) * part_heads,
                    lambda c: near_k[side, :, c], lambda c: near_v[side, :, c], near_bias,
                )

    def far_valid(offsets):
        pieces = [
            jnp.full((1, SUB), jnp.where(inside(me + offset), 0.0, NEG), jnp.float32)
            for offset in offsets
        ]
        return jnp.concatenate(pieces, axis=1)

    for slot, offset in enumerate(far_offsets):
        @pl.when(inside(me + offset))
        def _():
            far_copy(slot, offset, 0).wait_recv()
            far_copy(slot, offset, 1).wait_recv()
    far_copy(long_slot, steps[2], 0).wait_recv()
    far_copy(long_slot, steps[2], 1).wait_recv()
    shift = jnp.concatenate([far_valid(far_offsets), jnp.zeros((1, SUB), jnp.float32)], axis=1)
    sweep(0, heads, lambda c: far_k[:, c], lambda c: far_v[:, c], lambda tile: shift, last=True)

    each_near(lambda copy: copy.wait_send())
    for slot, offset, column in sends:
        @pl.when(inside(me - offset))
        def _():
            far_copy(slot, offset, 0).wait_send()
            far_copy(slot, offset, 1).wait_send()


def body(query_in, keys_in, values_in, far_picks, win_rows):
    frames = lax.axis_size("frame")
    _, tokens, width = query_in.shape
    heads = width // HD
    kind = query_in.dtype
    slots = 5 * SUB
    return pl.pallas_call(
        functools.partial(kernel, frames),
        out_shape=jax.ShapeDtypeStruct(query_in.shape, query_in.dtype),
        in_specs=[pl.BlockSpec(memory_space=pl.ANY)] * 3
        + [pl.BlockSpec(memory_space=pltpu.SMEM)] * 2,
        out_specs=pl.BlockSpec(memory_space=pltpu.VMEM),
        scratch_shapes=[
            pltpu.VMEM((tokens, width), kind),
            pltpu.VMEM((tokens, width), kind),
            pltpu.VMEM((tokens, width), kind),
            pltpu.VMEM((2, tokens, width), kind),
            pltpu.VMEM((2, tokens, width), kind),
            pltpu.VMEM((slots, width), kind),
            pltpu.VMEM((slots, width), kind),
            pltpu.VMEM((slots, width), kind),
            pltpu.VMEM((slots, width), kind),
            pltpu.VMEM((heads, tokens, HD), jnp.float32),
            pltpu.VMEM((heads, tokens, HD), jnp.float32),
            pltpu.VMEM((tokens, width), jnp.float32),
            pltpu.VMEM((tokens, tokens), jnp.float32),
            pltpu.SemaphoreType.DMA((3,)),
            pltpu.SemaphoreType.DMA((2, CHUNKS, 2)),
            pltpu.SemaphoreType.DMA((2, CHUNKS, 2)),
            pltpu.SemaphoreType.DMA((5, 2)),
            pltpu.SemaphoreType.DMA((5, 2)),
        ],
        compiler_params=pltpu.CompilerParams(
            collective_id=0, has_side_effects=True, vmem_limit_bytes=56 * 2**20
        ),
        cost_estimate=pl.CostEstimate(
            flops=4 * tokens * (3 * tokens + slots) * width,
            bytes_accessed=8 * tokens * width,
            transcendentals=heads * tokens * (3 * tokens + slots),
        ),
    )(query_in, keys_in, values_in, far_picks, win_rows)


def solution(mesh):
    in_specs = (
        P(("groups", "frame"), None, None),
        P(("groups", "frame"), None, None),
        P(("groups", "frame"), None, None),
        P("groups", None),
        P(("groups", "frame")),
    )
    out_specs = P(("groups", "frame"), None, None)
    return jax.shard_map(body, mesh=mesh, in_specs=in_specs, out_specs=out_specs, check_vma=False)
```

time: 248 us -> 125 us (0.50)
  the two profiles are of different devices: /device:TPU:1 before, /device:TPU:17 now
where the time goes in v1:
time: 125 us
  Pallas kernels  120 us (96%)
  local copies, waits for them, and re-layouts  4.01 us (3%)
    pallas_call x1, Pallas kernels, body(): pl.pallas_call(functools.partial(kernel, frames), out_shape=jax.ShapeDtyp...  120 us
    unnamed x2, local copies, waits for them, and re-layouts  4.01 us

profile of v1, /device:TPU:17, one launch (start us, length us, event | category | flops | bytes accessed | tf_op | source)
XLA Modules:
  0.0 125.1 jit_solution(4108967994216451062)
XLA Ops:
  0.7 1.4 %copy.6.picks = s32[16,6]{1,0:T(8,128)} copy(s32[16,6]{0,1:T(8,128)} %param.8) | data formatting | bytes 768 | tf_op args[3]
  2.0 120.5 %shard_map.55 = bf16[1,512,1536]{2,1,0:T(8,128)(2,1)} custom-call(bf16[1,512,1536]{2,1,0:T(8,128)(2,1)} %q_hbm.1, bf16[1,512,1536]{2,1,0:T(8,128)(2,1)} %k_hbm.1, bf16[1,512,1536]{2,1,0:T(8,128)(2,1)} %v_hbm.1, s32[16,6]{1,0:T(8,128)} %copy.6.picks, s32[1]{0:T(128)S(6)} %copy.8.win), custom_call_target="tpu_custom_call" | custom-call | flops 6845104128 | bytes 6291456 | tf_op jit(solution)/shard_map/pallas_call | solution.py:227
  122.5 2.7 %copy.9 = bf16[1,512,1536]{2,1,0:T(8,128)(2,1)} copy(bf16[1,512,1536]{2,1,0:T(8,128)(2,1)} %shard_map.55) | data formatting | bytes 3145728

commit v2 on v1

v2 whole, which is shorter than its diff:
```python
import functools
import math

import jax
import jax.numpy as jnp
from jax import lax
from jax.experimental import pallas as pl
from jax.experimental.pallas import tpu as pltpu
from jax.sharding import PartitionSpec as P

HD = 128
COLS = 32
SUB = 128
NREACH = 3
NEG = -1e30
CHUNKS = 3
TILE = 256
FACTOR = math.log2(math.e) / math.sqrt(HD)


def kernel(
    frames, q_hbm, k_hbm, v_hbm, picks, win, out_ref,
    qs, ks, vs, mate_k, mate_v, ext_k, ext_v, relay_k, relay_v,
    stage_k, stage_v, far_k, far_v,
    peak, total, acc, bias,
    in_sem, mate_send, mate_recv, ext_send, ext_recv, relay_send, relay_recv,
    far_send, far_recv, via_send, via_recv,
):
    tokens, width = qs.shape
    heads = width // HD
    part = width // CHUNKS
    part_heads = heads // CHUNKS
    units = 2 * CHUNKS
    group = lax.axis_index("groups")
    me = lax.axis_index("frame")
    steps = [frames // 2 ** (NREACH - j) for j in range(NREACH)]
    via_mate = steps[0] == 2
    quads = frames // 4 if frames % 4 == 0 else 0

    def inside(index):
        return (index >= 0) & (index < frames)

    odd = me % 2
    side = 2 * odd - 1
    mate = me - side
    outer = me + side
    has_outer = inside(outer)

    def relayed(sender):
        span = max(quads, 1)
        low = jnp.where(odd == 1, sender // 4, sender // 4 - 1)
        weight = jnp.where(odd == 1, span - 1 - low, low + 1)
        return jnp.minimum(units, (15 * weight + span) // (2 * span))

    place = me % 4
    if quads:
        crossing = ((place == 0) | (place == 3)) & has_outer
        is_relay = ((place == 1) | (place == 2)) & inside(me + 3 * side)
        my_relayed = jnp.where(crossing, relayed(me), 0)
        to_relay = jnp.where(is_relay, relayed(me + 2 * side), 0)
    else:
        crossing = place < 0
        my_relayed = to_relay = jnp.int32(0)

    loads = [
        pltpu.make_async_copy(src, dst, in_sem.at[i])
        for i, (src, dst) in enumerate(((k_hbm.at[0], ks), (v_hbm.at[0], vs), (q_hbm.at[0], qs)))
    ]
    for load in loads:
        load.start()

    barrier = pltpu.get_barrier_semaphore()
    count = jnp.int32(0)
    for distance in sorted({1, 2, 3, *steps}):
        for offset in (-distance, distance):
            ok = inside(me + offset)
            count = count + ok.astype(jnp.int32)

            @pl.when(ok)
            def _():
                pl.semaphore_signal(
                    barrier, inc=1, device_id=(group, me + offset),
                    device_id_type=pl.DeviceIdType.MESH,
                )
    pl.semaphore_wait(barrier, count)

    def remote(src, dst, send, recv, target):
        return pltpu.make_async_remote_copy(
            src_ref=src, dst_ref=dst, send_sem=send, recv_sem=recv,
            device_id=(group, target), device_id_type=pl.DeviceIdType.MESH,
        )

    def piece(unit):
        return pl.ds((unit // 2) * part, part)

    def mate_copy(unit):
        return remote(
            (k_hbm, v_hbm)[unit % 2].at[0, :, piece(unit)],
            (mate_k, mate_v)[unit % 2].at[:, piece(unit)],
            mate_send.at[unit], mate_recv.at[unit], mate,
        )

    def ext_copy(unit):
        return remote(
            (k_hbm, v_hbm)[unit % 2].at[0, :, piece(unit)],
            (ext_k, ext_v)[unit % 2].at[:, piece(unit)],
            ext_send.at[unit], ext_recv.at[unit], outer,
        )

    def to_relay_copy(unit):
        return remote(
            (k_hbm, v_hbm)[unit % 2].at[0, :, piece(unit)],
            (relay_k, relay_v)[unit % 2].at[:, piece(unit)],
            ext_send.at[unit], relay_recv.at[unit], me - 2 * side,
        )

    def relay_copy(unit):
        return remote(
            (relay_k, relay_v)[unit % 2].at[:, piece(unit)],
            (ext_k, ext_v)[unit % 2].at[:, piece(unit)],
            relay_send.at[unit], ext_recv.at[unit], me + 3 * side,
        )

    def far_copy(slot, target, kind):
        rows = pl.ds(slot * SUB, SUB)
        return remote(
            (stage_k, stage_v)[kind].at[rows, :], (far_k, far_v)[kind].at[rows, :],
            far_send.at[slot, kind], far_recv.at[slot, kind], target,
        )

    def via_copy(unit):
        rows = pl.ds(SUB, SUB)
        return remote(
            (stage_k, stage_v)[unit % 2].at[rows, piece(unit)],
            (far_k, far_v)[unit % 2].at[rows, piece(unit)],
            via_send.at[unit], via_recv.at[unit], mate,
        )

    def stage(slot, pick, src_k, src_v, low, high):
        chosen = jnp.broadcast_to(pick, (16, HD))
        hot = [
            jnp.concatenate(
                [jnp.where(chosen == block, 1.0, 0.0).astype(stage_k.dtype)] * (SUB // 16), axis=0
            )
            for block in range(tokens // SUB)
        ]

        def one_head(head, carry):
            columns = pl.ds(pl.multiple_of(head * HD, HD), HD)
            for src, dst in ((src_k, stage_k), (src_v, stage_v)):
                mixed = hot[0] * src[pl.ds(0, SUB), columns]
                for block in range(1, tokens // SUB):
                    mixed = mixed + hot[block] * src[pl.ds(block * SUB, SUB), columns]
                dst[pl.ds(slot * SUB, SUB), columns] = mixed
            return carry
        lax.fori_loop(low, high, one_head, 0)

    long_sends = [
        (4, me + steps[2], NREACH - 1), (4, me - steps[2], 2 * NREACH - 1),
        (2, me + steps[1], 1), (3, me - steps[1], NREACH + 1),
    ]
    short_sends = [(0, me - steps[0] * side, NREACH * odd)]
    if not via_mate:
        short_sends.append((1, me + steps[0] * side, NREACH * (1 - odd)))
    long_sources = [(2, me - steps[1]), (3, me + steps[1])]
    short_sources = [(0, me + steps[0] * side), (1, me - steps[0] * side)]

    def send_far(sends):
        for slot, reader, column in sends:
            @pl.when(inside(reader))
            def _():
                stage(slot, picks[reader, column], ks, vs, 0, heads)
                far_copy(slot, reader, 0).start()
                far_copy(slot, reader, 1).start()

    for unit in range(units):
        @pl.when(crossing & (unit < my_relayed))
        def _():
            to_relay_copy(unit).start()

        @pl.when(crossing & (unit >= my_relayed))
        def _():
            ext_copy(unit).start()
    for unit in range(units):
        mate_copy(unit).start()

    loads[0].wait()
    loads[1].wait()
    send_far(long_sends)

    for slot, source in long_sources + short_sources:
        @pl.when(jnp.logical_not(inside(source)))
        def _():
            rows = pl.ds(slot * SUB, SUB)
            far_k[rows, :] = jnp.zeros((SUB, width), far_k.dtype)
            far_v[rows, :] = jnp.zeros((SUB, width), far_v.dtype)

    reach = jnp.broadcast_to(win[0], (tokens, tokens))
    query_row = lax.broadcasted_iota(jnp.int32, (tokens, tokens), 0) // COLS
    key_row = lax.broadcasted_iota(jnp.int32, (tokens, tokens), 1) // COLS
    bias[...] = jnp.where(jnp.abs(query_row - key_row) <= reach, 0.0, NEG)
    loads[2].wait()

    def update(head, tile, key, value, shift, first, last):
        columns = pl.ds(pl.multiple_of(head * HD, HD), HD)
        rows = pl.ds(tile * TILE, TILE)
        scores = lax.dot_general(
            qs[rows, columns], key, (((1,), (1,)), ((), ())), preferred_element_type=jnp.float32
        )
        if shift is not None:
            scores = scores + shift
        lanes = scores.shape[1] // HD
        high = jnp.broadcast_to(jnp.max(scores, axis=1, keepdims=True), (TILE, HD))
        if not first:
            old = peak[head, rows, :]
            high = jnp.maximum(old, high)
            fade = jnp.exp2((old - high) * FACTOR)
        raw = jnp.exp2((scores - jnp.concatenate([high] * lanes, axis=1)) * FACTOR)
        summed = raw[:, :HD]
        for lane in range(1, lanes):
            summed = summed + raw[:, lane * HD:(lane + 1) * HD]
        weighted = jnp.dot(raw.astype(jnp.bfloat16), value, preferred_element_type=jnp.float32)
        if not first:
            summed = summed + fade * total[head, rows, :]
            weighted = weighted + fade * acc[rows, columns]
        if last:
            row_total = jnp.sum(summed, axis=1, keepdims=True)
            out_ref[0, rows, columns] = (weighted / row_total).astype(out_ref.dtype)
        else:
            peak[head, rows, :] = high
            total[head, rows, :] = summed
            acc[rows, columns] = weighted

    def sweep(low, high, keys, values, shift_for, first=False, last=False):
        def one_head(head, carry):
            columns = pl.ds(pl.multiple_of(head * HD, HD), HD)
            key, value = keys(columns), values(columns)
            for tile in range(tokens // TILE):
                update(head, tile, key, value, shift_for(tile), first, last)
            return carry
        lax.fori_loop(low, high, one_head, 0)

    def near_bias(tile):
        return bias[pl.ds(tile * TILE, TILE), :]

    def start_direct():
        send_far(short_sends)
        for unit in range(units):
            @pl.when(has_outer & jnp.logical_not(crossing))
            def _():
                ext_copy(unit).start()

    def pass_on(unit):
        @pl.when(unit < to_relay)
        def _():
            to_relay_copy(unit).wait_recv()
            relay_copy(unit).start()

    def far_shift(sources):
        pieces = [
            jnp.full((1, SUB), jnp.where(inside(source), 0.0, NEG), jnp.float32)
            for _, source in sources
        ]
        return jnp.concatenate(pieces, axis=1)

    sweep(0, heads, lambda c: ks[:, c], lambda c: vs[:, c], near_bias, first=True)
    pass_on(0)
    for chunk in range(CHUNKS):
        mate_copy(2 * chunk).wait_recv()
        mate_copy(2 * chunk + 1).wait_recv()
        sweep(
            chunk * part_heads, (chunk + 1) * part_heads,
            lambda c: mate_k[:, c], lambda c: mate_v[:, c], near_bias,
        )
        if chunk == 0:
            start_direct()
        pass_on(chunk + 1)

    for slot, source in long_sources:
        @pl.when(inside(source))
        def _():
            far_copy(slot, me, 0).wait_recv()
            far_copy(slot, me, 1).wait_recv()
    far_copy(4, me, 0).wait_recv()
    far_copy(4, me, 1).wait_recv()
    long_shift = jnp.concatenate([far_shift(long_sources), jnp.zeros((1, SUB), jnp.float32)], axis=1)
    long_rows = pl.ds(2 * SUB, 3 * SUB)
    sweep(0, heads, lambda c: far_k[long_rows, c], lambda c: far_v[long_rows, c], lambda tile: long_shift)
    for unit in range(CHUNKS + 1, units):
        pass_on(unit)

    short_shift = far_shift(short_sources)
    short_rows = pl.ds(0, 2 * SUB)
    for slot, source in short_sources[:1] if via_mate else short_sources:
        @pl.when(inside(source))
        def _():
            far_copy(slot, me, 0).wait_recv()
            far_copy(slot, me, 1).wait_recv()
    for chunk in range(CHUNKS):
        low, high = chunk * part_heads, (chunk + 1) * part_heads

        @pl.when(has_outer)
        def _():
            ext_copy(2 * chunk).wait_recv()
            ext_copy(2 * chunk + 1).wait_recv()
            if via_mate:
                stage(1, picks[mate, NREACH * odd], ext_k, ext_v, low, high)
                via_copy(2 * chunk).start()
                via_copy(2 * chunk + 1).start()
            sweep(low, high, lambda c: ext_k[:, c], lambda c: ext_v[:, c], near_bias)

        if via_mate:
            @pl.when(inside(me - 2 * side))
            def _():
                via_copy(2 * chunk).wait_recv()
                via_copy(2 * chunk + 1).wait_recv()
        sweep(
            low, high, lambda c: far_k[short_rows, c], lambda c: far_v[short_rows, c],
            lambda tile: short_shift, last=True,
        )

    for unit in range(units):
        mate_copy(unit).wait_send()

        @pl.when(has_outer)
        def _():
            ext_copy(unit).wait_send()
            if via_mate:
                via_copy(unit).wait_send()

        @pl.when(unit < to_relay)
        def _():
            relay_copy(unit).wait_send()
    for slot, reader, column in long_sends + short_sends:
        @pl.when(inside(reader))
        def _():
            far_copy(slot, reader, 0).wait_send()
            far_copy(slot, reader, 1).wait_send()


def body(query_in, keys_in, values_in, far_picks, win_rows):
    frames = lax.axis_size("frame")
    _, tokens, width = query_in.shape
    heads = width // HD
    kind = query_in.dtype
    slots = 5 * SUB
    return pl.pallas_call(
        functools.partial(kernel, frames),
        out_shape=jax.ShapeDtypeStruct(query_in.shape, query_in.dtype),
        in_specs=[pl.BlockSpec(memory_space=pl.ANY)] * 3
        + [pl.BlockSpec(memory_space=pltpu.SMEM)] * 2,
        out_specs=pl.BlockSpec(memory_space=pltpu.VMEM),
        scratch_shapes=[pltpu.VMEM((tokens, width), kind)] * 9
        + [pltpu.VMEM((slots, width), kind)] * 4
        + [pltpu.VMEM((heads, tokens, HD), jnp.float32)] * 2
        + [pltpu.VMEM((tokens, width), jnp.float32), pltpu.VMEM((tokens, tokens), jnp.float32)]
        + [pltpu.SemaphoreType.DMA((3,))]
        + [pltpu.SemaphoreType.DMA((2 * CHUNKS,))] * 6
        + [pltpu.SemaphoreType.DMA((5, 2))] * 2
        + [pltpu.SemaphoreType.DMA((2 * CHUNKS,))] * 2,
        compiler_params=pltpu.CompilerParams(
            collective_id=0, has_side_effects=True, vmem_limit_bytes=56 * 2**20
        ),
        cost_estimate=pl.CostEstimate(
            flops=4 * tokens * (3 * tokens + slots) * width,
            bytes_accessed=8 * tokens * width,
            transcendentals=heads * tokens * (3 * tokens + slots),
        ),
    )(query_in, keys_in, values_in, far_picks, win_rows)


def solution(mesh):
    in_specs = (
        P(("groups", "frame"), None, None),
        P(("groups", "frame"), None, None),
        P(("groups", "frame"), None, None),
        P("groups", None),
        P(("groups", "frame")),
    )
    out_specs = P(("groups", "frame"), None, None)
    return jax.shard_map(body, mesh=mesh, in_specs=in_specs, out_specs=out_specs, check_vma=False)
```

time: 125 us -> 110 us (0.88)
  the two profiles are of different devices: /device:TPU:17 before, /device:TPU:8 now
where the time goes in v2:
time: 110 us
  Pallas kernels  105 us (95%)
  local copies, waits for them, and re-layouts  4.01 us (4%)
    pallas_call x1, Pallas kernels, body(): pl.pallas_call(functools.partial(kernel, frames), out_shape=jax.ShapeDtyp...  105 us
    unnamed x2, local copies, waits for them, and re-layouts  4.01 us

profile of v2, /device:TPU:8, one launch (start us, length us, event | category | flops | bytes accessed | tf_op | source)
XLA Modules:
  0.0 109.8 jit_solution(1121893364984270226)
XLA Ops:
  0.7 1.4 %copy.6.picks = s32[16,6]{1,0:T(8,128)} copy(s32[16,6]{0,1:T(8,128)} %param.8) | data formatting | bytes 768 | tf_op args[3]
  2.0 105.2 %shard_map.55 = bf16[1,512,1536]{2,1,0:T(8,128)(2,1)} custom-call(bf16[1,512,1536]{2,1,0:T(8,128)(2,1)} %q_hbm.1, bf16[1,512,1536]{2,1,0:T(8,128)(2,1)} %k_hbm.1, bf16[1,512,1536]{2,1,0:T(8,128)(2,1)} %v_hbm.1, s32[16,6]{1,0:T(8,128)} %copy.6.picks, s32[1]{0:T(128)S(6)} %copy.8.win), custom_call_target="tpu_custom_call" | custom-call | flops 6845104128 | bytes 6291456 | tf_op jit(solution)/shard_map/pallas_call | solution.py:347
  107.2 2.7 %copy.9 = bf16[1,512,1536]{2,1,0:T(8,128)(2,1)} copy(bf16[1,512,1536]{2,1,0:T(8,128)(2,1)} %shard_map.55) | data formatting | bytes 3145728

commit v3 on v2

--- a/solution.py
+++ b/solution.py
@@ -173,14 +173,17 @@
                 far_copy(slot, reader, 0).start()
                 far_copy(slot, reader, 1).start()
 
-    for unit in range(units):
-        @pl.when(crossing & (unit < my_relayed))
-        def _():
-            to_relay_copy(unit).start()
-
-        @pl.when(crossing & (unit >= my_relayed))
-        def _():
-            ext_copy(unit).start()
+    def start_crossing(chunk):
+        for unit in (2 * chunk, 2 * chunk + 1):
+            @pl.when(crossing & (unit < my_relayed))
+            def _():
+                to_relay_copy(unit).start()
+
+            @pl.when(crossing & (unit >= my_relayed))
+            def _():
+                ext_copy(unit).start()
+
+    start_crossing(0)
     for unit in range(units):
         mate_copy(unit).start()
 
@@ -243,9 +246,8 @@
     def near_bias(tile):
         return bias[pl.ds(tile * TILE, TILE), :]
 
-    def start_direct():
-        send_far(short_sends)
-        for unit in range(units):
+    def start_direct(chunk):
+        for unit in (2 * chunk, 2 * chunk + 1):
             @pl.when(has_outer & jnp.logical_not(crossing))
             def _():
                 ext_copy(unit).start()
@@ -263,7 +265,11 @@
         ]
         return jnp.concatenate(pieces, axis=1)
 
-    sweep(0, heads, lambda c: ks[:, c], lambda c: vs[:, c], near_bias, first=True)
+    sweep(0, 2 * part_heads, lambda c: ks[:, c], lambda c: vs[:, c], near_bias, first=True)
+    start_crossing(1)
+    sweep(2 * part_heads, heads, lambda c: ks[:, c], lambda c: vs[:, c], near_bias, first=True)
+    send_far(short_sends)
+    start_direct(0)
     pass_on(0)
     for chunk in range(CHUNKS):
         mate_copy(2 * chunk).wait_recv()
@@ -273,7 +279,10 @@
             lambda c: mate_k[:, c], lambda c: mate_v[:, c], near_bias,
         )
         if chunk == 0:
-            start_direct()
+            start_crossing(2)
+            start_direct(1)
+        if chunk == 2:
+            start_direct(2)
         pass_on(chunk + 1)
 
     for slot, source in long_sources:

time: 110 us -> 104 us (0.945)
  the two profiles are of different devices: /device:TPU:8 before, /device:TPU:1 now
where the time goes in v3:
time: 104 us; the launch traced here: 103 us
  Pallas kernels  98.8 us (95%)
  local copies, waits for them, and re-layouts  4.01 us (4%)
    pallas_call x1, Pallas kernels, body(): pl.pallas_call(functools.partial(kernel, frames), out_shape=jax.ShapeDtyp...  98.8 us
    unnamed x2, local copies, waits for them, and re-layouts  4.01 us

profile of v3, /device:TPU:1, one launch (start us, length us, event | category | flops | bytes accessed | tf_op | source)
XLA Modules:
  0.0 103.5 jit_solution(4834420051076378602)
XLA Ops:
  0.7 1.4 %copy.6.picks = s32[16,6]{1,0:T(8,128)} copy(s32[16,6]{0,1:T(8,128)} %param.8) | data formatting | bytes 768 | tf_op args[3]
  2.0 98.8 %shard_map.55 = bf16[1,512,1536]{2,1,0:T(8,128)(2,1)} custom-call(bf16[1,512,1536]{2,1,0:T(8,128)(2,1)} %q_hbm.1, bf16[1,512,1536]{2,1,0:T(8,128)(2,1)} %k_hbm.1, bf16[1,512,1536]{2,1,0:T(8,128)(2,1)} %v_hbm.1, s32[16,6]{1,0:T(8,128)} %copy.6.picks, s32[1]{0:T(128)S(6)} %copy.8.win), custom_call_target="tpu_custom_call" | custom-call | flops 6845104128 | bytes 6291456 | tf_op jit(solution)/shard_map/pallas_call | solution.py:356
  100.8 2.7 %copy.9 = bf16[1,512,1536]{2,1,0:T(8,128)(2,1)} copy(bf16[1,512,1536]{2,1,0:T(8,128)(2,1)} %shard_map.55) | data formatting | bytes 3145728
